TPU v7x, 256 devices: a whole 4x4x8 slice. The times are simulated.
256 devices in a mesh: wave: 64 (over x, z, core), lev: 4 (over y).
Axes of the slice: x: 4, y: 4, z: 8, core: 2. Of those that a mesh axis runs over, the one named last changes fastest.
Arguments:
- spectral: float32 [64, 128, 2, 1280], P('wave', 'lev'), may hold values from -6 to 6
- legendre: bfloat16 [64, 1280, 1280], P('wave'), may hold values from -0.15625 to 0.15625
- gauss_weight: float32 [1280], replicated, may hold values from 0.5 to 2
- slot_waves: int32 [64], replicated, may hold values from 0 to 63, each once
- grid_factor: float32 [2560, 4096], P('wave'), may hold values from -6 to 6
- mode_projector: float32 [128, 128], replicated, may hold values from -1 to 2
- vertical_modes: float32 [128, 128], replicated, may hold values from -1 to 2
- mode_rates: float32 [128], replicated, may hold values from 0.05 to 5
Outputs:
- advanced: float32 [64, 128, 2, 1280], P('wave', 'lev')
Inputs may be any that keep to these rules, and one draw needn't show every extreme that they name: slot_waves holds every number of 0 to 63 once.
All inputs are finite; a program needn't handle non-finite values.
Results may differ from a plain program's by a relative error of at most 0.0051.
Values may be sent and summed in bfloat16 or wider, within the bound.
A program may use at most 64 MiB of HBM per device.

v0:
```python
import math

import jax
import jax.numpy as jnp
from jax import lax
from jax.sharding import PartitionSpec as P

time_step = 0.5
square_weight = 0.3


def local(
    spectral,
    legendre,
    gauss_weight,
    slot_waves,
    grid_factor,
    mode_projector,
    vertical_modes,
    mode_rates,
):
    local_slots, lev_local, _, orders = spectral.shape
    half = legendre.shape[1]
    nlon = grid_factor.shape[1]
    total_slots = slot_waves.shape[0]
    stride = ((orders - 1) // (total_slots - 1) - 1) // 2 * 2 + 1
    width = 2 * lev_local
    owned = lax.dynamic_slice_in_dim(slot_waves, lax.axis_index("wave") * local_slots, local_slots)
    waves = owned * stride
    order_index = jnp.arange(orders, dtype=jnp.int32)
    live = (order_index[None, :] < (orders - waves)[:, None]).astype(jnp.float32)
    parity = jnp.where(order_index % 2 == 0, 1.0, -1.0).astype(jnp.float32)
    masked = spectral * live[:, None, None, :]
    coeffs = masked.reshape(local_slots, width, orders).astype(jnp.bfloat16)
    stacked = jnp.concatenate([coeffs, coeffs * parity.astype(jnp.bfloat16)], axis=1)
    fields = jnp.einsum("shk,sck->shc", legendre, stacked, preferred_element_type=jnp.float32)
    fourier = jnp.concatenate([fields[:, :, :width], fields[:, ::-1, width:]], axis=1)
    fourier = fourier.astype(jnp.bfloat16).reshape(local_slots, 2 * half, lev_local, 2)
    all_waves = slot_waves * stride
    longitude = jnp.arange(nlon, dtype=jnp.int32)
    phase = all_waves[:, None] * longitude[None, :] % nlon
    angle = phase.astype(jnp.float32) * (2.0 * math.pi / nlon)
    table = jnp.stack([jnp.cos(angle), -jnp.sin(angle)], axis=1).astype(jnp.bfloat16)
    root_scale = 1.0 / math.sqrt(total_slots)
    lon_scale = 1.0 / math.sqrt(nlon)
    part = lax.all_to_all(fourier, "wave", split_axis=1, concat_axis=0, tiled=True)
    slots, band, levels, _ = part.shape
    block = math.gcd(band, 8)
    count = band // block
    blocks = part.reshape(slots, count, block, levels, 2).transpose(1, 0, 2, 3, 4)
    factors = grid_factor.reshape(count, block, nlon)

    def one_block(args):
        piece, factor = args
        grid = (
            jnp.einsum("sbvr,srl->bvl", piece, table, preferred_element_type=jnp.float32)
            * root_scale
        )
        product = (factor[:, None, :] * grid + square_weight * grid * grid).astype(jnp.bfloat16)
        analysed = (
            jnp.einsum("bvl,srl->sbvr", product, table, preferred_element_type=jnp.float32)
            * lon_scale
        )
        return analysed.astype(jnp.bfloat16)

    analysed_all = lax.map(one_block, (blocks, factors))
    analysed_all = analysed_all.transpose(1, 0, 2, 3, 4).reshape(slots, band, levels, 2)
    returned = lax.all_to_all(analysed_all, "wave", split_axis=0, concat_axis=1, tiled=True)
    north = returned[:, :half].reshape(local_slots, half, width).astype(jnp.float32)
    south = returned[:, half:][:, ::-1].reshape(local_slots, half, width).astype(jnp.float32)
    weighted = (jnp.concatenate([north, south], axis=2) * gauss_weight[None, :, None]).astype(
        jnp.bfloat16
    )
    sums = jnp.einsum("shk,shc->sck", legendre, weighted, preferred_element_type=jnp.float32)
    tendency = sums[:, :width] + parity[None, None, :] * sums[:, width:]
    tendency = tendency.reshape(local_slots, lev_local, 2, orders) * live[:, None, None, :]
    rhs = masked + time_step * tendency
    degree = (waves[:, None] + order_index[None, :]).astype(jnp.float32)
    damping = degree * (degree + 1.0) / float(orders * orders)
    start_lev = lax.axis_index("lev") * lev_local
    own_columns = lax.dynamic_slice_in_dim(mode_projector, start_lev, lev_local, 1)
    flat_rhs = rhs.transpose(1, 0, 2, 3).reshape(lev_local, local_slots * 2 * orders)
    chosen = own_columns
    share = lax.psum_scatter(
        jnp.dot(
            chosen, flat_rhs, precision=lax.Precision.HIGHEST, preferred_element_type=jnp.float32
        ),
        "lev",
        scatter_dimension=0,
        tiled=True,
    )
    rates_here = lax.dynamic_slice_in_dim(mode_rates, start_lev, lev_local)
    share = share.reshape(lev_local, local_slots, 2, orders)
    share = share / (1.0 + rates_here[:, None, None, None] * damping[None, :, None, :])
    flat_share = share.reshape(lev_local, local_slots * 2 * orders)
    own_rows = lax.dynamic_slice_in_dim(vertical_modes, start_lev, lev_local, 0)
    chosen = own_rows
    summed = jnp.dot(
        chosen,
        lax.all_gather(flat_share, "lev", axis=0, tiled=True),
        precision=lax.Precision.HIGHEST,
        preferred_element_type=jnp.float32,
    )
    advanced = summed.reshape(lev_local, local_slots, 2, orders).transpose(1, 0, 2, 3)
    return advanced


def solution(mesh):
    in_specs = (
        P("wave", "lev", None, None),
        P("wave", None, None),
        P(),
        P(),
        P("wave", None),
        P(),
        P(),
        P(),
    )
    out_specs = P("wave", "lev", None, None)
    return jax.shard_map(local, mesh=mesh, in_specs=in_specs, out_specs=out_specs, check_vma=False)
```

profile of v0, /device:TPU:2, one launch (start us, length us, event | category | flops | bytes accessed | tf_op | source)
XLA Modules:
  0.0 217.0 jit_solution(14931276656885235147)
XLA Ops:
  13.3 5.6 %rev.6 = bf16[1,1280,64]{1,2,0:T(8,128)(2,1)} reverse(bf16[1,1280,64]{1,2,0:T(8,128)(2,1)} %get-tuple-element.104), dimensions={1} | reverse | bytes 327680 | tf_op jit(solution)/shard_map/rev | solution.py:37
  20.5 2.8 %copy.34 = bf16[1,1280,32,2]{2,3,0,1:T(2,128)(2,1)} copy(bf16[1,1280,32,2]{1,3,2,0:T(2,128)(2,1)} %concatenate.48) | data formatting | bytes 327680 | tf_op jit(solution)/shard_map/concatenate | solution.py:37
  24.0 2.8 %copy.33 = bf16[1,1280,32,2]{2,3,0,1:T(2,128)(2,1)} copy(bf16[1,1280,32,2]{1,3,2,0:T(2,128)(2,1)} %concatenate.47) | data formatting | bytes 327680 | tf_op jit(solution)/shard_map/concatenate | solution.py:37
  26.8 7.1 %fusion.59 = bf16[2560,1,2,32]{3,2,1,0:T(2,128)(2,1)} fusion(bf16[1,1280,32,2]{2,3,0,1:T(2,128)(2,1)} %copy.34, bf16[1,1280,32,2]{2,3,0,1:T(2,128)(2,1)} %copy.33), kind=kLoop, calls=%fused_computation.73 | loop fusion | flops 163840 | bytes 655360
  33.9 4.4 %reshape.431 = bf16[64,2,1280]{2,1,0:T(2,128)(2,1)} reshape(bf16[2560,1,2,32]{3,2,1,0:T(2,128)(2,1)} %fusion.59) | data formatting | bytes 655360
  38.2 12.2 %all-to-all-start = ((bf16[64,2,1280]{2,1,0:T(2,128)(2,1)}), bf16[64,2,1280]{2,1,0:T(2,128)(2,1)}, u32[]{:S(2)}, u32[]{:S(2)}) async-start(bf16[64,2,1280]{2,1,0:T(2,128)(2,1)} %reshape.431), calls=%async_computation | async-start | bytes 655360 | tf_op jit(solution)/shard_map/all_to_all | solution.py:46
  50.5 5.7 %cosine_convert_fusion = (bf16[64,1,4096]{2,0,1:T(8,128)(2,1)}, bf16[64,1,4096]{2,0,1:T(8,128)(2,1)}) fusion(s32[64]{0:T(128)S(1)} %broadcast_multiply_fusion.1), kind=kLoop, calls=%fused_computation.30 | loop fusion | flops 4456448 | bytes 1048832 | tf_op jit(solution)/shard_map/convert.3
  56.2 2.3 %pad_maximum_fusion.1 = bf16[64,2,4096]{2,0,1:T(8,128)(2,1)} fusion(bf16[64,1,4096]{2,0,1:T(8,128)(2,1)} %get-tuple-element.106, bf16[64,1,4096]{2,0,1:T(8,128)(2,1)} %get-tuple-element.105), kind=kLoop, calls=%fused_computation.28 | loop fusion | flops 524288 | bytes 2097152 | tf_op jit(solution)/shard_map/stack | solution.py:43
  58.5 4.8 %all-to-all-done = bf16[64,2,1280]{2,1,0:T(2,128)(2,1)} async-done(((bf16[64,2,1280]{2,1,0:T(2,128)(2,1)}), bf16[64,2,1280]{2,1,0:T(2,128)(2,1)}, u32[]{:S(2)}, u32[]{:S(2)}) %all-to-all-start) | async-done | bytes 327712 | tf_op jit(solution)/shard_map/all_to_all | solution.py:46
  63.2 4.4 %reshape.432 = bf16[2560,1,2,32]{3,2,1,0:T(2,128)(2,1)} reshape(bf16[64,2,1280]{2,1,0:T(2,128)(2,1)} %all-to-all-done) | data formatting | bytes 655360
  67.6 2.6 %copy.35 = bf16[1,2560,32,2]{2,1,3,0:T(8,128)(2,1)} copy(bf16[1,2560,32,2]{2,3,0,1:T(2,128)(2,1)} %bitcast.115) | data formatting | bytes 655360 | tf_op jit(solution)/shard_map/all_to_all | solution.py:46
  70.1 2.5 %copy.36 = bf16[5,64,8,32,2]{1,3,4,2,0:T(8,128)(2,1)} copy(bf16[5,64,8,32,2]{3,2,0,1,4:T(8,128)(2,1)} %bitcast.116) | data formatting | bytes 655360 | tf_op jit(solution)/shard_map/while | solution.py:66
  72.7 22.9 %while.12 = (s32[]{:T(128)}, bf16[5,64,8,32,2]{1,3,4,2,0:T(8,128)(2,1)}, bf16[5,64,8,32,2]{1,3,4,2,0:T(8,128)(2,1)}, bf16[64,2,4096]{2,0,1:T(8,128)(2,1)}, f32[5,8,4096]{2,1,0:T(8,128)}, /*index=5*/s32[]{:T(128)}) while((s32[]{:T(128)}, bf16[5,64,8,32,2]{1,3,4,2,0:T(8,128)(2,1)}, bf16[5,64,8,32,2]{1,3,4,2,0:T(8,128)(2,1)}, ...), condition=%wide.region_1.2_spmd, body=%wide.region_0.1_spmd.sunk | while | flops 543260672 | bytes 2753609 | solution.py:66
  73.6 3.7 %fusion.69 = bf16[5,64,8,32,2]{1,3,4,2,0:T(8,128)(2,1)} fusion(bf16[5,64,8,32,2]{1,3,4,2,0:T(8,128)(2,1)} %get-tuple-element.145, s32[]{:T(128)} %get-tuple-element.144, f32[8,4096]{1,0:T(8,128)S(1)} %multiply_bitcast_fusion.2, bf16[64,2,4096]{2,0,1:T(8,128)(2,1)} %get-tuple-element.153, bf16[5,64,8,32,2]{1,3,4,2,0:T(8,128)(2,1)} %get-tuple-element.152), kind=kOutput, calls=%fused_computation.7.clone.1 | convolution fusion | flops 543227904 | bytes 2491392 | tf_op jit(solution)/shard_map/while/body/eval_jaxpr/bvl,srl->sbvr/dot_general | solution.py:61
  78.2 3.7 %fusion.69 = bf16[5,64,8,32,2]{1,3,4,2,0:T(8,128)(2,1)} fusion(bf16[5,64,8,32,2]{1,3,4,2,0:T(8,128)(2,1)} %get-tuple-element.145, s32[]{:T(128)} %get-tuple-element.144, f32[8,4096]{1,0:T(8,128)S(1)} %multiply_bitcast_fusion.2, bf16[64,2,4096]{2,0,1:T(8,128)(2,1)} %get-tuple-element.153, bf16[5,64,8,32,2]{1,3,4,2,0:T(8,128)(2,1)} %get-tuple-element.152), kind=kOutput, calls=%fused_computation.7.clone.1 | convolution fusion | flops 543227904 | bytes 2491392 | tf_op jit(solution)/shard_map/while/body/eval_jaxpr/bvl,srl->sbvr/dot_general | solution.py:61
  82.7 3.7 %fusion.69 = bf16[5,64,8,32,2]{1,3,4,2,0:T(8,128)(2,1)} fusion(bf16[5,64,8,32,2]{1,3,4,2,0:T(8,128)(2,1)} %get-tuple-element.145, s32[]{:T(128)} %get-tuple-element.144, f32[8,4096]{1,0:T(8,128)S(1)} %multiply_bitcast_fusion.2, bf16[64,2,4096]{2,0,1:T(8,128)(2,1)} %get-tuple-element.153, bf16[5,64,8,32,2]{1,3,4,2,0:T(8,128)(2,1)} %get-tuple-element.152), kind=kOutput, calls=%fused_computation.7.clone.1 | convolution fusion | flops 543227904 | bytes 2491392 | tf_op jit(solution)/shard_map/while/body/eval_jaxpr/bvl,srl->sbvr/dot_general | solution.py:61
  87.3 3.7 %fusion.69 = bf16[5,64,8,32,2]{1,3,4,2,0:T(8,128)(2,1)} fusion(bf16[5,64,8,32,2]{1,3,4,2,0:T(8,128)(2,1)} %get-tuple-element.145, s32[]{:T(128)} %get-tuple-element.144, f32[8,4096]{1,0:T(8,128)S(1)} %multiply_bitcast_fusion.2, bf16[64,2,4096]{2,0,1:T(8,128)(2,1)} %get-tuple-element.153, bf16[5,64,8,32,2]{1,3,4,2,0:T(8,128)(2,1)} %get-tuple-element.152), kind=kOutput, calls=%fused_computation.7.clone.1 | convolution fusion | flops 543227904 | bytes 2491392 | tf_op jit(solution)/shard_map/while/body/eval_jaxpr/bvl,srl->sbvr/dot_general | solution.py:61
  91.9 3.7 %fusion.69 = bf16[5,64,8,32,2]{1,3,4,2,0:T(8,128)(2,1)} fusion(bf16[5,64,8,32,2]{1,3,4,2,0:T(8,128)(2,1)} %get-tuple-element.145, s32[]{:T(128)} %get-tuple-element.144, f32[8,4096]{1,0:T(8,128)S(1)} %multiply_bitcast_fusion.2, bf16[64,2,4096]{2,0,1:T(8,128)(2,1)} %get-tuple-element.153, bf16[5,64,8,32,2]{1,3,4,2,0:T(8,128)(2,1)} %get-tuple-element.152), kind=kOutput, calls=%fused_computation.7.clone.1 | convolution fusion | flops 543227904 | bytes 2491392 | tf_op jit(solution)/shard_map/while/body/eval_jaxpr/bvl,srl->sbvr/dot_general | solution.py:61
  95.6 3.7 %copy.37 = bf16[64,40,32,2]{1,2,3,0:T(8,128)(2,1)} copy(bf16[64,40,32,2]{0,2,3,1:T(8,128)(2,1)} %bitcast.124) | data formatting | bytes 655360 | tf_op jit(solution)/shard_map/reshape | solution.py:67
  99.3 3.6 %reshape.433 = bf16[64,2,1280]{2,1,0:T(2,128)(2,1)} reshape(bf16[64,2,32,40]{3,2,1,0:T(8,128)(2,1)} %bitcast.118) | data formatting | bytes 655360
  102.9 6.7 %all-to-all-start.1 = ((bf16[64,2,1280]{2,1,0:T(2,128)(2,1)}), bf16[64,2,1280]{2,1,0:T(2,128)(2,1)}, u32[]{:S(2)}, u32[]{:S(2)}) async-start(bf16[64,2,1280]{2,1,0:T(2,128)(2,1)} %reshape.433), calls=%async_computation.1 | async-start | bytes 655360 | tf_op jit(solution)/shard_map/all_to_all | solution.py:68
  110.0 12.5 %all-to-all-done.1 = bf16[64,2,1280]{2,1,0:T(2,128)(2,1)} async-done(((bf16[64,2,1280]{2,1,0:T(2,128)(2,1)}), bf16[64,2,1280]{2,1,0:T(2,128)(2,1)}, u32[]{:S(2)}, u32[]{:S(2)}) %all-to-all-start.1) | async-done | bytes 327712 | tf_op jit(solution)/shard_map/all_to_all | solution.py:68
  122.4 3.7 %reshape.434 = bf16[64,2,32,40]{3,2,1,0:T(8,128)(2,1)} reshape(bf16[64,2,1280]{2,1,0:T(2,128)(2,1)} %all-to-all-done.1) | data formatting | bytes 655360
  126.1 2.9 %copy.38 = bf16[64,40,32,2]{1,0,2,3:T(8,128)(2,1)} copy(bf16[64,40,32,2]{1,2,3,0:T(8,128)(2,1)} %bitcast.117) | data formatting | bytes 655360 | tf_op jit(solution)/shard_map/all_to_all | solution.py:68
  129.0 3.2 %all_to_all.8 = bf16[1,2560,32,2]{1,2,3,0:T(8,128)(2,1)} reshape(bf16[64,40,32,2]{1,0,2,3:T(8,128)(2,1)} %copy.38) | data formatting | bytes 655360 | tf_op jit(solution)/shard_map/all_to_all | solution.py:68
  133.9 3.5 %rev.7 = bf16[1,1280,32,2]{1,2,3,0:T(8,128)(2,1)} reverse(bf16[1,1280,32,2]{1,2,3,0:T(8,128)(2,1)S(1)} %get-tuple-element.102), dimensions={1} | reverse | bytes 327680 | tf_op jit(solution)/shard_map/rev | solution.py:70
  145.9 1.9 reshape.427
  149.1 2.3 %fusion.41 = f32[128,2560]{1,0:T(8,128)} fusion(f32[32,2560]{1,0:T(8,128)S(1)} %bitcast.122, f32[128,128]{1,0:T(8,128)S(1)} %copy-done.1, s32[]{:T(128)S(6)} %select_n.54), kind=kOutput, calls=%fused_computation.50 | convolution fusion | flops 125829120 | bytes 1703940 | tf_op jit(solution)/shard_map/dot_general | solution.py:85
  152.6 23.6 %reduce-scatter.2.cloned.1.call-done = f32[32,2560]{1,0:T(8,128)} async-done(((f32[128,2560]{1,0:T(8,128)}), f32[32,2560]{1,0:T(8,128)}) %reduce-scatter.2.cloned.1.call-update) | async-done | bytes 327696 | tf_op jit(solution)/shard_map/reduce_scatter | solution.py:84
  178.0 27.4 %all-gather.2.cloned.1.call-done = f32[128,2560]{1,0:T(8,128)} async-done(((f32[32,2560]{1,0:T(8,128)}), f32[128,2560]{1,0:T(8,128)}) %all-gather.2.cloned.1.call-update) | async-done | bytes 1310736 | tf_op jit(solution)/shard_map/all_gather | solution.py:100
  205.4 2.8 %fusion.43 = f32[32,2560]{1,0:T(8,128)} fusion(f32[128,2560]{1,0:T(8,128)} %all-gather.2.cloned.1.call-done, f32[128,128]{1,0:T(8,128)} %param.16, s32[]{:T(128)S(6)} %select_n.54), kind=kOutput, calls=%fused_computation.52 | convolution fusion | flops 125829120 | bytes 1654788 | tf_op jit(solution)/shard_map/dot_general | solution.py:98
  208.2 1.9 transpose_reshape.3
  (47 shorter events, 27.7 us)
Async XLA Ops:
  6.5 4.8 %copy-start = (bf16[1,1280,1280]{2,1,0:T(8,128)(2,1)S(1)}, bf16[1,1280,1280]{2,1,0:T(8,128)(2,1)}, u32[]{:S(2)}) copy-start(bf16[1,1280,1280]{2,1,0:T(8,128)(2,1)} %param.11) | copy-start | bytes 9830404
  20.5 30.0 %copy-start.3 = (s32[64]{0:T(128)S(1)}, s32[64]{0:T(128)}, u32[]{:S(2)}) copy-start(s32[64]{0:T(128)} %param.13) | copy-start | bytes 772
  38.2 25.0 %all-to-all-start = ((bf16[64,2,1280]{2,1,0:T(2,128)(2,1)}), bf16[64,2,1280]{2,1,0:T(2,128)(2,1)}, u32[]{:S(2)}, u32[]{:S(2)}) async-start(bf16[64,2,1280]{2,1,0:T(2,128)(2,1)} %reshape.431), calls=%async_computation | async-start | bytes 655360 | tf_op jit(solution)/shard_map/all_to_all | solution.py:46
  102.9 19.5 %all-to-all-start.1 = ((bf16[64,2,1280]{2,1,0:T(2,128)(2,1)}), bf16[64,2,1280]{2,1,0:T(2,128)(2,1)}, u32[]{:S(2)}, u32[]{:S(2)}) async-start(bf16[64,2,1280]{2,1,0:T(2,128)(2,1)} %reshape.433), calls=%async_computation.1 | async-start | bytes 655360 | tf_op jit(solution)/shard_map/all_to_all | solution.py:68
  109.7 66.5 %reduce-scatter.2.cloned.1.call-start = ((), (), s32[]{:S(2)}) async-start(), calls=%async_computation.3 | async-start | bytes 1638400 | tf_op jit(solution)/shard_map/reduce_scatter | solution.py:84
  109.9 33.6 %copy-start.2 = (f32[1280]{0:T(1024)S(1)}, f32[1280]{0:T(1024)}, u32[]{:S(2)}) copy-start(f32[1280]{0:T(1024)} %param.12) | copy-start | bytes 15364
  143.6 5.5 %copy-start.1 = (f32[128,128]{1,0:T(8,128)S(1)}, f32[128,128]{1,0:T(8,128)}, u32[]{:S(2)}) copy-start(f32[128,128]{1,0:T(8,128)} %param.15) | copy-start | bytes 196612
  145.1 6.4 %copy-start.4 = (f32[128]{0:T(128)S(1)}, f32[128]{0:T(128)}, u32[]{:S(2)}) copy-start(f32[128]{0:T(128)} %param.17) | copy-start | bytes 1540
  151.5 53.9 %all-gather.2.cloned.1.call-start = ((), (), s32[]{:S(2)}) async-start(), calls=%async_computation.4 | async-start | bytes 1638400 | tf_op jit(solution)/shard_map/all_gather | solution.py:100
Sparse Core Ops, SparseCore 0:
  151.6 24.5 reduce-scatter.1
  178.1 27.2 all-gather.1
where the time goes:
time: 219 us; the launch traced here: 217 us
  waiting for transfers between devices  68.2 us (31%)
  local copies, waits for them, and re-layouts  63.6 us (29%)
  matrix products  26.2 us (12%)
  other arithmetic  25.4 us (12%)
  starting transfers between devices  19.2 us (9%)
  between operations  14.2 us (6%)
    all_gather x1, waiting for transfers between devices, local(): lax.all_gather(flat_share, 'lev', axis=0, tiled=True)  27.4 us
    reduce_scatter x1, waiting for transfers between devices, local(): lax.psum_scatter(jnp.dot(chosen, flat_rhs, precision=lax.Precision.HIGHES...  23.6 us
    dot_general x5, matrix products, one_block(): jnp.einsum('bvl,srl->sbvr', product, table, preferred_element_type=jnp.fl...  18.3 us
    unnamed x16, local copies, waits for them, and re-layouts  16.8 us
    all_to_all x1, waiting for transfers between devices, local(): lax.all_to_all(analysed_all, 'wave', split_axis=0, concat_axis=1, tiled=T...  12.5 us
    all_to_all x1, starting transfers between devices, local(): lax.all_to_all(fourier, 'wave', split_axis=1, concat_axis=0, tiled=True)  12.2 us
    concatenate x4, local copies, waits for them, and re-layouts, local(): jnp.concatenate([fields[:, :, :width], fields[:, ::-1, width:]], axis=1)  7.95 us
    unnamed x1, other arithmetic  7.08 us
  transfers between devices with their start and end apart: 4, of which 4 were waited for; matrix products, arithmetic and copies ran while one was open for 4% of the time, Pallas kernels for 0%

commit v1 on v0

v1 whole, which is shorter than its diff:
```python
import functools
import math

import jax
import jax.numpy as jnp
import numpy as np
from jax import lax
from jax.experimental import pallas as pl
from jax.experimental.pallas import tpu as pltpu
from jax.sharding import PartitionSpec as P

time_step = 0.5
square_weight = 0.3
MESH = pl.DeviceIdType.MESH
f32, bf16 = jnp.float32, jnp.bfloat16
HIGHEST = lax.Precision.HIGHEST


@functools.lru_cache(maxsize=None)
def tables(slots, nlon, stride):
    points = 4 * slots
    step = nlon // points
    m = (np.arange(nlon, dtype=np.int64) * stride) % nlon
    i = np.arange(points, dtype=np.int64) * step
    q = np.arange(1, 2 * slots)
    series = 1.0 + 2.0 * np.cos(2.0 * np.pi * np.outer(np.arange(nlon), q) / nlon).sum(1)
    kernel = series[(m[None, :] - i[:, None]) % nlon] / nlon
    high = kernel.astype(np.float32).astype(jnp.bfloat16)
    low = (kernel - high.astype(np.float64)).astype(np.float32).astype(jnp.bfloat16)
    smooth = np.stack([part.T.reshape(nlon, -1, 128) for part in (high, low)], axis=1)
    smooth = np.ascontiguousarray(smooth.transpose(1, 2, 0, 3)).reshape(-1, nlon, 128)
    angle = 2.0 * np.pi * (np.outer(np.arange(points), np.arange(slots)) % points) / points
    waves = np.concatenate([np.cos(angle), -np.sin(angle)], axis=1)
    return smooth, waves.astype(np.float32).astype(jnp.bfloat16)


def dot(a, b, contract, precision=None):
    return lax.dot_general(
        a, b, (contract, ((), ())), precision=precision, preferred_element_type=f32
    )


def kernel(
    cfg,
    spec_h,
    leg_h,
    gw_h,
    sw_h,
    fac_h,
    mp_h,
    vm_h,
    mr_h,
    smooth_h,
    waves_h,
    out_ref,
    spec,
    leg,
    gw,
    sw,
    sw_s,
    fac,
    mp,
    vm,
    mr,
    smooth,
    waves,
    in_sem,
    leg_sem,
    own_sem,
    mask_out,
    mask_in,
    still_out,
    still_in,
    tend_out,
    tend_in,
    move_out,
    move_in,
    to_grid,
    at_grid,
    to_slot,
    at_slot,
    field,
    rows32,
    gwb,
    damp,
    fbig,
    trig,
    trig_t,
    lev_send,
    lev_recv,
    wave_send,
    wave_recv,
):
    slots, levs, half, orders, nlon, band, stride = cfg
    vl = spec.shape[0]
    lanes = 128
    groups = lanes // vl
    tiles = band // groups
    bands = half // band
    points = waves.shape[0]
    kq = orders // 2
    w = lax.axis_index("wave")
    y = lax.axis_index("lev")
    rows = 2 * tiles

    def load(src, dst, sem):
        cp = pltpu.make_async_copy(src, dst, sem)
        cp.start()
        return cp

    spec_cp = load(spec_h, spec, in_sem.at[0])
    sws_cp = load(sw_h, sw_s, in_sem.at[1])
    pieces = 5
    piece = half // pieces
    leg_cps = [
        load(leg_h.at[pl.ds(i * piece, piece)], leg.at[pl.ds(i * piece, piece)], leg_sem.at[i])
        for i in range(pieces)
    ]
    others = [
        load(a, b, in_sem.at[2 + i])
        for i, (a, b) in enumerate(
            [
                (sw_h, sw),
                (waves_h, waves),
                (gw_h, gw),
                (mr_h, mr),
                (mp_h, mp),
                (vm_h, vm),
                (fac_h, fac),
                (smooth_h, smooth),
            ]
        )
    ]

    barrier = pltpu.get_barrier_semaphore()

    def greet(i, _):
        pl.semaphore_signal(
            barrier, inc=1, device_id=(lax.rem(w + i, slots), y), device_id_type=MESH
        )
        return 0

    lax.fori_loop(1, slots, greet, 0)
    for i in range(1, levs):
        pl.semaphore_signal(
            barrier, inc=1, device_id=(w, lax.rem(y + i, levs)), device_id_type=MESH
        )

    sws_cp.wait()
    spec_cp.wait()
    wave = sw_s[w] * stride
    order = lax.broadcasted_iota(jnp.int32, (1, orders), 1)
    live = jnp.where(order < orders - wave, 1.0, 0.0).astype(f32)
    parity = jnp.where(order % 2 == 0, 1.0, -1.0).astype(f32)
    masked = [spec[:, r, :] * live for r in range(2)]
    for r in range(2):
        for h in range(2):
            mask_out[2 * r + h] = masked[r][:, h * kq : (h + 1) * kq]
    coeffs = jnp.concatenate(masked, axis=0)
    coeffs = jnp.concatenate([coeffs, coeffs * parity], axis=0).astype(bf16)
    for i in range(pieces):
        leg_cps[i].wait()
        field[pl.ds(i * piece, piece), :] = dot(
            leg[pl.ds(i * piece, piece), :], coeffs, ((1,), (1,))
        )

    lane = lax.broadcasted_iota(jnp.int32, (bands * tiles, lanes), 1) // vl

    def pick(parts, shift):
        acc = None
        for b in range(groups):
            turn = (shift(b) * vl) % lanes
            part = pltpu.roll(parts[b], turn, 1) if turn else parts[b]
            acc = part if acc is None else jnp.where(lane == b, part, acc)
        return acc

    block = bands * tiles
    cut = [field[pl.ds(a, block, stride=groups), :] for a in range(groups)]
    for n in range(2):
        for r in range(2):
            q = 2 * n + r
            rows32[pl.ds(n * 2 * block + r, block, stride=2), :] = pick(cut, lambda a: a - q)
    to_grid[...] = rows32[...].astype(bf16).reshape(to_grid.shape)

    pl.semaphore_wait(barrier, slots - 1 + levs - 1)

    def place(d):
        return d + (d // bands) * (3 * bands - 1 - 2 * d)

    def forward(i, _):
        d = lax.rem(w + i, slots)
        pltpu.make_async_remote_copy(
            src_ref=to_grid.at[place(d)],
            dst_ref=at_grid.at[w],
            send_sem=wave_send.at[0],
            recv_sem=wave_recv.at[0],
            device_id=(d, y),
            device_id_type=MESH,
        ).start()
        return 0

    lax.fori_loop(1, slots, forward, 0)
    own = pltpu.make_async_copy(to_grid.at[place(w)], at_grid.at[w], own_sem.at[0])
    own.start()

    def across(src, dst, k):
        cps = []
        for i in range(1, levs):
            to = lax.rem(y + i, levs)
            cp = pltpu.make_async_remote_copy(
                src_ref=src.at[to],
                dst_ref=dst.at[y],
                send_sem=lev_send.at[k, i - 1],
                recv_sem=lev_recv.at[k, i - 1],
                device_id=(w, to),
                device_id_type=MESH,
            )
            cp.start()
            cps.append(cp)
        dst[y] = src[y]
        return cps

    first = across(mask_out, mask_in, 0)

    for cp in others:
        cp.wait()
    for i in range(half // lanes):
        gwb[pl.ds(i * lanes, lanes), :] = jnp.broadcast_to(
            gw[pl.ds(i * lanes, lanes)].reshape(1, lanes), (lanes, lanes)
        ).T
    part_j = lax.broadcasted_iota(jnp.int32, (2 * slots, slots), 0)
    held = jnp.broadcast_to(sw[...].reshape(1, slots), (2 * slots, slots))
    choose = jnp.concatenate(
        [jnp.where(part_j == held + r * slots, 1.0, 0.0) for r in range(2)], axis=1
    ).astype(bf16)
    turned = dot(waves[...], choose, ((1,), (0,)))
    trig[...] = turned.astype(bf16)
    trig_t[...] = turned.T.astype(bf16)

    factor = fac[...]
    fhigh = factor.astype(bf16)
    flow = (factor - fhigh.astype(f32)).astype(bf16)
    half_points = points // lanes
    shigh, slow = [
        jnp.concatenate([smooth[n * half_points + i] for i in range(half_points)], axis=1)
        for n in range(2)
    ]
    top = dot(fhigh, shigh, ((1,), (0,))) + dot(flow, shigh, ((1,), (0,)))
    top += dot(fhigh, slow, ((1,), (0,)))
    root = 1.0 / math.sqrt(slots)
    top = top * root
    thigh = top.astype(bf16)
    tlow = (top - thigh.astype(f32)).astype(bf16)
    row = lax.broadcasted_iota(jnp.int32, (band, tiles * lanes), 0)
    south = w // bands
    row = row + south * (band - 1 - 2 * row)
    col = lax.broadcasted_iota(jnp.int32, (band, tiles * lanes), 1) // vl
    spread = jnp.where(row == col, 1.0, 0.0).astype(bf16)
    fbig[...] = dot(thigh, spread, ((0,), (0,))) + dot(tlow, spread, ((0,), (0,)))

    total = (wave + (y % 2) * kq + lax.broadcasted_iota(jnp.int32, (1, kq), 1)).astype(f32)
    damping = total * (total + 1.0) / float(orders * orders)
    rates = jnp.broadcast_to(mr[...].reshape(1, lanes), (lanes, lanes)).T[:, :1]
    damp[...] = 1.0 / (1.0 + rates * damping)

    def solve(x):
        modes = dot(mp[...], x, ((1,), (0,)), HIGHEST) * damp[...]
        return dot(vm[...], modes, ((1,), (0,)), HIGHEST)

    for cp in first:
        cp.wait()
    still_out[...] = solve(mask_in[...].reshape(levs * vl, kq)).reshape(levs, vl, kq)
    second = across(still_out, still_in, 1)

    own.wait()
    pltpu.make_async_copy(
        at_grid.at[pl.ds(0, slots - 1)], at_grid.at[pl.ds(0, slots - 1)], wave_recv.at[0]
    ).wait()
    rows32[...] = at_grid[...].reshape(slots * rows, lanes).astype(f32)
    for t in range(0, tiles, 2):
        piece_t = jnp.concatenate(
            [
                jnp.concatenate(
                    [rows32[pl.ds(2 * u + r, slots, stride=rows), :] for r in range(2)], axis=0
                )
                for u in (t, t + 1)
            ],
            axis=1,
        ).astype(bf16)
        grid = dot(trig[...], piece_t, ((1,), (0,)))
        fac_t = fbig[:, t * lanes : (t + 2) * lanes]
        product = (grid * (fac_t + (square_weight * root * root) * grid)).astype(bf16)
        back = dot(trig_t[...], product, ((1,), (0,)))
        back = back * ((nlon // points) / math.sqrt(nlon))
        for u in (t, t + 1):
            for r in range(2):
                field[pl.ds(2 * u + r, slots, stride=rows), :] = back[
                    r * slots : (r + 1) * slots, (u - t) * lanes : (u - t + 1) * lanes
                ]
    to_slot[...] = field[...].astype(bf16).reshape(to_slot.shape)

    def backward(i, _):
        d = lax.rem(w + i, slots)
        pltpu.make_async_remote_copy(
            src_ref=to_slot.at[d],
            dst_ref=at_slot.at[place(w)],
            send_sem=wave_send.at[1],
            recv_sem=wave_recv.at[1],
            device_id=(d, y),
            device_id_type=MESH,
        ).start()
        return 0

    lax.fori_loop(1, slots, backward, 0)
    own = pltpu.make_async_copy(to_slot.at[w], at_slot.at[place(w)], own_sem.at[1])
    own.start()
    own.wait()
    pltpu.make_async_copy(
        at_slot.at[pl.ds(0, slots - 1)], at_slot.at[pl.ds(0, slots - 1)], wave_recv.at[1]
    ).wait()

    rows32[...] = at_slot[...].reshape(slots * rows, lanes).astype(f32)
    cut = [
        rows32[pl.ds(n * 2 * block + r, block, stride=2), :] for n in range(2) for r in range(2)
    ]
    for a in range(groups):
        field[pl.ds(a, block, stride=groups), :] = pick(cut, lambda q: q - a)
    weighted = (field[...] * gwb[...]).astype(bf16)
    sums = dot(weighted, leg[...], ((0,), (0,)))
    tend = (sums[: 2 * vl] + parity * sums[2 * vl :]) * (live * time_step)
    for r in range(2):
        for h in range(2):
            tend_out[2 * r + h] = tend[r * vl : (r + 1) * vl, h * kq : (h + 1) * kq].astype(bf16)
    third = across(tend_out, tend_in, 2)
    for cp in third:
        cp.wait()
    change = tend_in[...].reshape(levs * vl, kq).astype(f32)
    move_out[...] = solve(change).reshape(levs, vl, kq).astype(bf16)
    fourth = across(move_out, move_in, 3)
    for cp in second:
        cp.wait()
    for cp in fourth:
        cp.wait()
    for r in range(2):
        for h in range(2):
            out_ref[:, r, h * kq : (h + 1) * kq] = still_in[2 * r + h] + move_in[
                2 * r + h
            ].astype(f32)
    for k, buf in ((0, to_grid), (1, to_slot)):
        pltpu.make_async_copy(
            buf.at[pl.ds(0, slots - 1)], buf.at[pl.ds(0, slots - 1)], wave_send.at[k]
        ).wait()


def local(
    spectral,
    legendre,
    gauss_weight,
    slot_waves,
    grid_factor,
    mode_projector,
    vertical_modes,
    mode_rates,
):
    _, vl, _, orders = spectral.shape
    half = legendre.shape[1]
    band, nlon = grid_factor.shape
    slots = slot_waves.shape[0]
    nmodes = mode_rates.shape[0]
    levs = nmodes // vl
    stride = ((orders - 1) // (slots - 1) - 1) // 2 * 2 + 1
    smooth, waves = tables(slots, nlon, stride)
    points = waves.shape[0]
    kq = orders // 2
    lanes = 128
    groups = lanes // vl
    tiles = band // groups
    cfg = (slots, levs, half, orders, nlon, band, stride)
    vmem = pltpu.VMEM
    dma = pltpu.SemaphoreType.DMA
    cells = vmem((slots, tiles, 2, lanes), bf16)
    scratch = [
        vmem((vl, 2, orders), f32),
        vmem((half, orders), bf16),
        vmem((half,), f32),
        vmem((slots,), jnp.int32),
        pltpu.SMEM((slots,), jnp.int32),
        vmem((band, nlon), f32),
        vmem((nmodes, nmodes), f32),
        vmem((nmodes, nmodes), f32),
        vmem((nmodes,), f32),
        vmem(smooth.shape, bf16),
        vmem(waves.shape, bf16),
        dma((10,)),
        dma((5,)),
        dma((2,)),
        vmem((levs, vl, kq), f32),
        vmem((levs, vl, kq), f32),
        vmem((levs, vl, kq), f32),
        vmem((levs, vl, kq), f32),
        vmem((levs, vl, kq), bf16),
        vmem((levs, vl, kq), bf16),
        vmem((levs, vl, kq), bf16),
        vmem((levs, vl, kq), bf16),
        cells,
        cells,
        cells,
        cells,
        vmem((half, lanes), f32),
        vmem((half, lanes), f32),
        vmem((half, lanes), f32),
        vmem((nmodes, kq), f32),
        vmem((points, tiles * lanes), f32),
        vmem((points, 2 * slots), bf16),
        vmem((2 * slots, points), bf16),
        dma((4, levs - 1)),
        dma((4, levs - 1)),
        dma((2,)),
        dma((2,)),
    ]
    out = pl.pallas_call(
        functools.partial(kernel, cfg),
        out_shape=jax.ShapeDtypeStruct((vl, 2, orders), f32),
        in_specs=[pl.BlockSpec(memory_space=pl.ANY)] * 10,
        out_specs=pl.BlockSpec(memory_space=vmem),
        scratch_shapes=scratch,
        compiler_params=pltpu.CompilerParams(
            collective_id=0, has_side_effects=True, vmem_limit_bytes=56 * 2**20
        ),
        name="round_trip",
    )(
        spectral[0],
        legendre[0],
        gauss_weight,
        slot_waves,
        grid_factor,
        mode_projector,
        vertical_modes,
        mode_rates,
        jnp.asarray(smooth),
        jnp.asarray(waves),
    )
    return out[None]


def solution(mesh):
    in_specs = (
        P("wave", "lev", None, None),
        P("wave", None, None),
        P(),
        P(),
        P("wave", None),
        P(),
        P(),
        P(),
    )
    out_specs = P("wave", "lev", None, None)
    return jax.shard_map(local, mesh=mesh, in_specs=in_specs, out_specs=out_specs, check_vma=False)
```

time: 219 us -> 46.9 us (0.21)
  waiting for transfers between devices: 68.2 us -> 0 us
  local copies, waits for them, and re-layouts: 63.6 us -> 1.73 us
  Pallas kernels: 0 us -> 44.6 us
  matrix products: 26.2 us -> 0 us
  other arithmetic: 25.4 us -> 0 us
  starting transfers between devices: 19.2 us -> 0 us
  between operations: 14.2 us -> 0.01 us
    pallas_call x0 -> x1, Pallas kernels: none -> 44.6 us  [local(): pl.pallas_call(functools.partial(kernel, cfg), out_shape=jax.ShapeDtypeSt...]
    all_gather x1 -> x0, waiting for transfers between devices: 27.4 us -> none  [local(): lax.all_gather(flat_share, 'lev', axis=0, tiled=True)]
    dot_general x9 -> x0, matrix products: 26.2 us -> none  [the longest x5 18.3 us: one_block(): jnp.einsum('bvl,srl->sbvr', product, table, preferred_element_type=jnp.fl...]
    reduce_scatter x1 -> x0, waiting for transfers between devices: 23.6 us -> none  [local(): lax.psum_scatter(jnp.dot(chosen, flat_rhs, precision=lax.Precision.HIGHES...]
    all_to_all x2 -> x0, starting transfers between devices: 18.9 us -> none  [the longest x1 12.2 us: local(): lax.all_to_all(fourier, 'wave', split_axis=1, concat_axis=0, tiled=True)]
    all_to_all x2 -> x0, waiting for transfers between devices: 17.3 us -> none  [the longest x1 12.5 us: local(): lax.all_to_all(analysed_all, 'wave', split_axis=0, concat_axis=1, tiled=T...]
    unnamed x16 -> x1, local copies, waits for them, and re-layouts: 16.8 us -> 1.73 us
    rev x3 -> x0, local copies, waits for them, and re-layouts: 10.8 us -> none  [the longest x1 5.56 us: local(): fields[:, ::-1, width:]]
  transfers between devices with their start and end apart: 4 -> 0, of which waited for: 4 -> 0; matrix products, arithmetic and copies ran while one was open for 4% -> 0% of each run, Pallas kernels for 0% -> 0%
where the time goes in v1:
time: 46.9 us; the launch traced here: 46.3 us
  Pallas kernels  44.6 us (95%)
  local copies, waits for them, and re-layouts  1.73 us (4%)
    pallas_call x1, Pallas kernels, local(): pl.pallas_call(functools.partial(kernel, cfg), out_shape=jax.ShapeDtypeSt...  44.6 us
    unnamed x1, local copies, waits for them, and re-layouts  1.73 us

profile of v1, /device:TPU:2, one launch (start us, length us, event | category | flops | bytes accessed | tf_op | source)
XLA Modules:
  0.0 46.3 jit_solution(1684551485950921294)
XLA Ops:
  0.0 44.6 %round_trip.1 = f32[32,2,1280]{2,1,0:T(2,128)} custom-call(f32[32,2,1280]{2,1,0:T(2,128)} %bitcast.5, bf16[1280,1280]{1,0:T(8,128)(2,1)} %bitcast.3, f32[1280]{0:T(1024)} %gw_h.1, s32[64]{0:T(128)} %sw_h.1, f32[40,4096]{1,0:T(8,128)} %fac_h.1, f32[128,128]{1,0:T(8,128)} %mp_h.1, f32[128,128]{1,0:T(8,128)} %vm_h.1, f32[128]{0:T(128)} %mr_h.1, ...), custom_call_target="tpu_custom_call" | custom-call | tf_op jit(solution)/shard_map/round_trip/pallas_call | solution.py:421
  44.6 1.7 %copy.12 = f32[1,32,2,1280]{3,2,1,0:T(2,128)} copy(f32[1,32,2,1280]{3,2,1,0:T(2,128)} %bitcast.4) | data formatting | bytes 655360

commit v2 on v1

--- a/solution.py
+++ b/solution.py
@@ -86,12 +86,13 @@
     fbig,
     trig,
     trig_t,
+    pair,
     lev_send,
     lev_recv,
     wave_send,
     wave_recv,
 ):
-    slots, levs, half, orders, nlon, band, stride = cfg
+    slots, levs, half, orders, nlon, band, stride, cuts = cfg
     vl = spec.shape[0]
     lanes = 128
     groups = lanes // vl
@@ -187,19 +188,20 @@
     def place(d):
         return d + (d // bands) * (3 * bands - 1 - 2 * d)
 
-    def forward(i, _):
+    def forward(c, i, _):
         d = lax.rem(w + i, slots)
         pltpu.make_async_remote_copy(
-            src_ref=to_grid.at[place(d)],
-            dst_ref=at_grid.at[w],
-            send_sem=wave_send.at[0],
-            recv_sem=wave_recv.at[0],
+            src_ref=to_grid.at[place(d), pl.ds(*cuts[c])],
+            dst_ref=at_grid.at[w, pl.ds(*cuts[c])],
+            send_sem=wave_send.at[0, c],
+            recv_sem=wave_recv.at[0, c],
             device_id=(d, y),
             device_id_type=MESH,
         ).start()
         return 0
 
-    lax.fori_loop(1, slots, forward, 0)
+    for c in range(len(cuts)):
+        lax.fori_loop(1, slots, functools.partial(forward, c), 0)
     own = pltpu.make_async_copy(to_grid.at[place(w)], at_grid.at[w], own_sem.at[0])
     own.start()
 
@@ -267,57 +269,77 @@
         modes = dot(mp[...], x, ((1,), (0,)), HIGHEST) * damp[...]
         return dot(vm[...], modes, ((1,), (0,)), HIGHEST)
 
+    def split(x):
+        high = x.astype(bf16)
+        return high, (x - high.astype(f32)).astype(bf16)
+
+    ends = [split(ref[...]) for ref in (mp, vm)]
+    for k in range(2):
+        pair[k] = jnp.concatenate(ends[k], axis=1)
+
+    def solve_change(x):
+        modes = dot(pair[0], jnp.concatenate([x, x], axis=0), ((1,), (0,))) * damp[...]
+        high, low = split(modes)
+        out = dot(pair[1], jnp.concatenate([high, high], axis=0), ((1,), (0,)))
+        return out + dot(pair[1, :, :lanes], low, ((1,), (0,)))
+
     for cp in first:
         cp.wait()
     still_out[...] = solve(mask_in[...].reshape(levs * vl, kq)).reshape(levs, vl, kq)
     second = across(still_out, still_in, 1)
 
-    own.wait()
-    pltpu.make_async_copy(
-        at_grid.at[pl.ds(0, slots - 1)], at_grid.at[pl.ds(0, slots - 1)], wave_recv.at[0]
-    ).wait()
-    rows32[...] = at_grid[...].reshape(slots * rows, lanes).astype(f32)
-    for t in range(0, tiles, 2):
-        piece_t = jnp.concatenate(
-            [
-                jnp.concatenate(
-                    [rows32[pl.ds(2 * u + r, slots, stride=rows), :] for r in range(2)], axis=0
-                )
-                for u in (t, t + 1)
-            ],
-            axis=1,
-        ).astype(bf16)
-        grid = dot(trig[...], piece_t, ((1,), (0,)))
-        fac_t = fbig[:, t * lanes : (t + 2) * lanes]
-        product = (grid * (fac_t + (square_weight * root * root) * grid)).astype(bf16)
-        back = dot(trig_t[...], product, ((1,), (0,)))
-        back = back * ((nlon // points) / math.sqrt(nlon))
-        for u in (t, t + 1):
-            for r in range(2):
-                field[pl.ds(2 * u + r, slots, stride=rows), :] = back[
-                    r * slots : (r + 1) * slots, (u - t) * lanes : (u - t + 1) * lanes
-                ]
-    to_slot[...] = field[...].astype(bf16).reshape(to_slot.shape)
-
-    def backward(i, _):
+    def await_all(buf, sems, c):
+        ref = buf.at[pl.ds(0, slots - 1), pl.ds(*cuts[c])]
+        pltpu.make_async_copy(ref, ref, sems.at[c]).wait()
+
+    def backward(c, i, _):
         d = lax.rem(w + i, slots)
         pltpu.make_async_remote_copy(
-            src_ref=to_slot.at[d],
-            dst_ref=at_slot.at[place(w)],
-            send_sem=wave_send.at[1],
-            recv_sem=wave_recv.at[1],
+            src_ref=to_slot.at[d, pl.ds(*cuts[c])],
+            dst_ref=at_slot.at[place(w), pl.ds(*cuts[c])],
+            send_sem=wave_send.at[1, c],
+            recv_sem=wave_recv.at[1, c],
             device_id=(d, y),
             device_id_type=MESH,
         ).start()
         return 0
 
-    lax.fori_loop(1, slots, backward, 0)
+    own.wait()
+    for c, (start, count) in enumerate(cuts):
+        await_all(at_grid, wave_recv.at[0], c)
+        chunk = 2 * count
+        here = pl.ds(0, slots * chunk)
+        rows32[here, :] = (
+            at_grid[:, start : start + count].reshape(slots * chunk, lanes).astype(f32)
+        )
+        parts = jnp.concatenate(
+            [
+                jnp.concatenate(
+                    [rows32[pl.ds(2 * u + r, slots, stride=chunk), :] for r in range(2)], axis=0
+                ).astype(bf16)
+                for u in range(count)
+            ],
+            axis=1,
+        )
+        grid = dot(trig[...], parts, ((1,), (0,)))
+        scaled = fbig[:, start * lanes : (start + count) * lanes]
+        product = (grid * (scaled + (square_weight * root * root) * grid)).astype(bf16)
+        back = dot(trig_t[...], product, ((1,), (0,)))
+        back = back * ((nlon // points) / math.sqrt(nlon))
+        for u in range(count):
+            for r in range(2):
+                field[pl.ds(2 * u + r, slots, stride=chunk), :] = back[
+                    r * slots : (r + 1) * slots, u * lanes : (u + 1) * lanes
+                ]
+        to_slot[:, start : start + count] = (
+            field[here, :].astype(bf16).reshape(slots, count, 2, lanes)
+        )
+        lax.fori_loop(1, slots, functools.partial(backward, c), 0)
     own = pltpu.make_async_copy(to_slot.at[w], at_slot.at[place(w)], own_sem.at[1])
     own.start()
     own.wait()
-    pltpu.make_async_copy(
-        at_slot.at[pl.ds(0, slots - 1)], at_slot.at[pl.ds(0, slots - 1)], wave_recv.at[1]
-    ).wait()
+    for c in range(len(cuts)):
+        await_all(at_slot, wave_recv.at[1], c)
 
     rows32[...] = at_slot[...].reshape(slots * rows, lanes).astype(f32)
     cut = [
@@ -334,8 +356,8 @@
     third = across(tend_out, tend_in, 2)
     for cp in third:
         cp.wait()
-    change = tend_in[...].reshape(levs * vl, kq).astype(f32)
-    move_out[...] = solve(change).reshape(levs, vl, kq).astype(bf16)
+    change = tend_in[...].reshape(levs * vl, kq)
+    move_out[...] = solve_change(change).reshape(levs, vl, kq).astype(bf16)
     fourth = across(move_out, move_in, 3)
     for cp in second:
         cp.wait()
@@ -347,9 +369,8 @@
                 2 * r + h
             ].astype(f32)
     for k, buf in ((0, to_grid), (1, to_slot)):
-        pltpu.make_async_copy(
-            buf.at[pl.ds(0, slots - 1)], buf.at[pl.ds(0, slots - 1)], wave_send.at[k]
-        ).wait()
+        for c in range(len(cuts)):
+            await_all(buf, wave_send.at[k], c)
 
 
 def local(
@@ -375,7 +396,9 @@
     lanes = 128
     groups = lanes // vl
     tiles = band // groups
-    cfg = (slots, levs, half, orders, nlon, band, stride)
+    first = tiles // 2
+    cuts = ((0, first), (first, tiles - first))
+    cfg = (slots, levs, half, orders, nlon, band, stride, cuts)
     vmem = pltpu.VMEM
     dma = pltpu.SemaphoreType.DMA
     cells = vmem((slots, tiles, 2, lanes), bf16)
@@ -413,14 +436,15 @@
         vmem((points, tiles * lanes), f32),
         vmem((points, 2 * slots), bf16),
         vmem((2 * slots, points), bf16),
+        vmem((2, nmodes, 2 * nmodes), bf16),
         dma((4, levs - 1)),
         dma((4, levs - 1)),
-        dma((2,)),
-        dma((2,)),
+        dma((2, len(cuts))),
+        dma((2, len(cuts))),
     ]
     out = pl.pallas_call(
         functools.partial(kernel, cfg),
-        out_shape=jax.ShapeDtypeStruct((vl, 2, orders), f32),
+        out_shape=pltpu.VMEM((vl, 2, orders), f32),
         in_specs=[pl.BlockSpec(memory_space=pl.ANY)] * 10,
         out_specs=pl.BlockSpec(memory_space=vmem),
         scratch_shapes=scratch,

time: 46.9 us -> 42 us (0.90)
  Pallas kernels: 44.6 us -> 41 us
  local copies, waits for them, and re-layouts: 1.73 us -> 0.73 us
    pallas_call x1, Pallas kernels: 44.6 us -> 41 us  [local(): pl.pallas_call(functools.partial(kernel, cfg), out_shape=pltpu.VMEM((vl,...]
    unnamed x1, local copies, waits for them, and re-layouts: 1.73 us -> 0.73 us
where the time goes in v2:
time: 42 us; the launch traced here: 41.7 us
  Pallas kernels  41 us (98%)
  local copies, waits for them, and re-layouts  0.73 us (2%)
    pallas_call x1, Pallas kernels, local(): pl.pallas_call(functools.partial(kernel, cfg), out_shape=pltpu.VMEM((vl,...  41 us

profile of v2, /device:TPU:2, one launch (start us, length us, event | category | flops | bytes accessed | tf_op | source)
XLA Modules:
  0.0 41.7 jit_solution(8701893131763994623)
XLA Ops:
  0.0 41.0 %round_trip.1 = f32[32,2,1280]{2,1,0:T(2,128)S(1)} custom-call(f32[32,2,1280]{2,1,0:T(2,128)} %bitcast.5, bf16[1280,1280]{1,0:T(8,128)(2,1)} %bitcast.4, f32[1280]{0:T(1024)} %gw_h.1, s32[64]{0:T(128)} %sw_h.1, f32[40,4096]{1,0:T(8,128)} %fac_h.1, f32[128,128]{1,0:T(8,128)} %mp_h.1, f32[128,128]{1,0:T(8,128)} %vm_h.1, f32[128]{0:T(128)} %mr_h.1, ...), custom_call_target="tpu_custom_call" | custom-call | tf_op jit(solution)/shard_map/round_trip/pallas_call | solution.py:445
  41.0 0.7 %copy.12 = f32[1,32,2,1280]{3,2,1,0:T(2,128)} copy(f32[1,32,2,1280]{3,2,1,0:T(2,128)S(1)} %bitcast.3) | data formatting | bytes 655360

commit v3 on v2

--- a/solution.py
+++ b/solution.py
@@ -34,6 +34,16 @@
     return smooth, waves.astype(np.float32).astype(jnp.bfloat16)
 
 
+@functools.lru_cache(maxsize=None)
+def swap_blocks(groups, size):
+    width = groups * groups * size
+    at = np.arange(width).reshape(groups, groups, size).transpose(1, 0, 2).reshape(-1)
+    swap = np.zeros((width, width), np.float32)
+    swap[at, np.arange(width)] = 1.0
+    swap = swap.reshape(width, -1, 128).transpose(1, 0, 2)
+    return np.ascontiguousarray(swap).astype(jnp.bfloat16)
+
+
 def dot(a, b, contract, precision=None):
     return lax.dot_general(
         a, b, (contract, ((), ())), precision=precision, preferred_element_type=f32
@@ -52,6 +62,7 @@
     mr_h,
     smooth_h,
     waves_h,
+    swap_h,
     out_ref,
     spec,
     leg,
@@ -64,6 +75,7 @@
     mr,
     smooth,
     waves,
+    swap,
     in_sem,
     leg_sem,
     own_sem,
@@ -82,6 +94,9 @@
     field,
     rows32,
     gwb,
+    gwbc,
+    legc,
+    partial,
     damp,
     fbig,
     trig,
@@ -92,7 +107,7 @@
     wave_send,
     wave_recv,
 ):
-    slots, levs, half, orders, nlon, band, stride, cuts = cfg
+    slots, levs, half, orders, nlon, band, stride, cuts, splits = cfg
     vl = spec.shape[0]
     lanes = 128
     groups = lanes // vl
@@ -104,12 +119,31 @@
     y = lax.axis_index("lev")
     rows = 2 * tiles
 
+    barrier = pltpu.get_barrier_semaphore()
+
+    def every_peer(act):
+        def step(i, _):
+            act(lax.rem(w + i, slots))
+            return 0
+
+        lax.fori_loop(1, slots, step, 0)
+
+    def greet(d):
+        pl.semaphore_signal(barrier, inc=1, device_id=(d, y), device_id_type=MESH)
+
+    every_peer(greet)
+    for i in range(1, levs):
+        pl.semaphore_signal(
+            barrier, inc=1, device_id=(w, lax.rem(y + i, levs)), device_id_type=MESH
+        )
+
     def load(src, dst, sem):
         cp = pltpu.make_async_copy(src, dst, sem)
         cp.start()
         return cp
 
     spec_cp = load(spec_h, spec, in_sem.at[0])
+    swap_cp = load(swap_h, swap, in_sem.at[10])
     sws_cp = load(sw_h, sw_s, in_sem.at[1])
     pieces = 5
     piece = half // pieces
@@ -133,20 +167,6 @@
         )
     ]
 
-    barrier = pltpu.get_barrier_semaphore()
-
-    def greet(i, _):
-        pl.semaphore_signal(
-            barrier, inc=1, device_id=(lax.rem(w + i, slots), y), device_id_type=MESH
-        )
-        return 0
-
-    lax.fori_loop(1, slots, greet, 0)
-    for i in range(1, levs):
-        pl.semaphore_signal(
-            barrier, inc=1, device_id=(w, lax.rem(y + i, levs)), device_id_type=MESH
-        )
-
     sws_cp.wait()
     spec_cp.wait()
     wave = sw_s[w] * stride
@@ -165,22 +185,22 @@
             leg[pl.ds(i * piece, piece), :], coeffs, ((1,), (1,))
         )
 
-    lane = lax.broadcasted_iota(jnp.int32, (bands * tiles, lanes), 1) // vl
-
-    def pick(parts, shift):
-        acc = None
-        for b in range(groups):
-            turn = (shift(b) * vl) % lanes
-            part = pltpu.roll(parts[b], turn, 1) if turn else parts[b]
-            acc = part if acc is None else jnp.where(lane == b, part, acc)
-        return acc
-
     block = bands * tiles
-    cut = [field[pl.ds(a, block, stride=groups), :] for a in range(groups)]
+    swap_cp.wait()
+
+    def swapped(parts):
+        turn = jnp.concatenate([swap[i] for i in range(groups)], axis=1)
+        return dot(jnp.concatenate(parts, axis=1), turn, ((1,), (0,)))
+
+    turned = swapped(
+        [field[pl.ds(a, block, stride=groups), :].astype(bf16) for a in range(groups)]
+    )
     for n in range(2):
         for r in range(2):
             q = 2 * n + r
-            rows32[pl.ds(n * 2 * block + r, block, stride=2), :] = pick(cut, lambda a: a - q)
+            rows32[pl.ds(n * 2 * block + r, block, stride=2), :] = turned[
+                :, q * lanes : (q + 1) * lanes
+            ]
     to_grid[...] = rows32[...].astype(bf16).reshape(to_grid.shape)
 
     pl.semaphore_wait(barrier, slots - 1 + levs - 1)
@@ -188,8 +208,7 @@
     def place(d):
         return d + (d // bands) * (3 * bands - 1 - 2 * d)
 
-    def forward(c, i, _):
-        d = lax.rem(w + i, slots)
+    def forward(c, d):
         pltpu.make_async_remote_copy(
             src_ref=to_grid.at[place(d), pl.ds(*cuts[c])],
             dst_ref=at_grid.at[w, pl.ds(*cuts[c])],
@@ -198,16 +217,15 @@
             device_id=(d, y),
             device_id_type=MESH,
         ).start()
-        return 0
 
     for c in range(len(cuts)):
-        lax.fori_loop(1, slots, functools.partial(forward, c), 0)
+        every_peer(functools.partial(forward, c))
     own = pltpu.make_async_copy(to_grid.at[place(w)], at_grid.at[w], own_sem.at[0])
     own.start()
 
     def across(src, dst, k):
         cps = []
-        for i in range(1, levs):
+        for i in (2, 1, 3):
             to = lax.rem(y + i, levs)
             cp = pltpu.make_async_remote_copy(
                 src_ref=src.at[to],
@@ -230,6 +248,14 @@
         gwb[pl.ds(i * lanes, lanes), :] = jnp.broadcast_to(
             gw[pl.ds(i * lanes, lanes)].reshape(1, lanes), (lanes, lanes)
         ).T
+    base = 0
+    for start, count in cuts:
+        size = count * groups
+        for i in range(bands):
+            src, dst = pl.ds(i * band + start * groups, size), pl.ds(base + i * size, size)
+            legc[dst, :] = leg[src, :]
+            gwbc[dst, :] = gwb[src, :]
+        base += bands * size
     part_j = lax.broadcasted_iota(jnp.int32, (2 * slots, slots), 0)
     held = jnp.broadcast_to(sw[...].reshape(1, slots), (2 * slots, slots))
     choose = jnp.concatenate(
@@ -277,8 +303,8 @@
     for k in range(2):
         pair[k] = jnp.concatenate(ends[k], axis=1)
 
-    def solve_change(x):
-        modes = dot(pair[0], jnp.concatenate([x, x], axis=0), ((1,), (0,))) * damp[...]
+    def solve_change(x, damping):
+        modes = dot(pair[0], jnp.concatenate([x, x], axis=0), ((1,), (0,))) * damping
         high, low = split(modes)
         out = dot(pair[1], jnp.concatenate([high, high], axis=0), ((1,), (0,)))
         return out + dot(pair[1, :, :lanes], low, ((1,), (0,)))
@@ -292,8 +318,7 @@
         ref = buf.at[pl.ds(0, slots - 1), pl.ds(*cuts[c])]
         pltpu.make_async_copy(ref, ref, sems.at[c]).wait()
 
-    def backward(c, i, _):
-        d = lax.rem(w + i, slots)
+    def backward(c, d):
         pltpu.make_async_remote_copy(
             src_ref=to_slot.at[d, pl.ds(*cuts[c])],
             dst_ref=at_slot.at[place(w), pl.ds(*cuts[c])],
@@ -302,7 +327,6 @@
             device_id=(d, y),
             device_id_type=MESH,
         ).start()
-        return 0
 
     own.wait()
     for c, (start, count) in enumerate(cuts):
@@ -334,40 +358,67 @@
         to_slot[:, start : start + count] = (
             field[here, :].astype(bf16).reshape(slots, count, 2, lanes)
         )
-        lax.fori_loop(1, slots, functools.partial(backward, c), 0)
+        every_peer(functools.partial(backward, c))
     own = pltpu.make_async_copy(to_slot.at[w], at_slot.at[place(w)], own_sem.at[1])
     own.start()
     own.wait()
-    for c in range(len(cuts)):
+    third = []
+    base = 0
+    for c, (start, count) in enumerate(cuts):
         await_all(at_slot, wave_recv.at[1], c)
-
-    rows32[...] = at_slot[...].reshape(slots * rows, lanes).astype(f32)
-    cut = [
-        rows32[pl.ds(n * 2 * block + r, block, stride=2), :] for n in range(2) for r in range(2)
-    ]
-    for a in range(groups):
-        field[pl.ds(a, block, stride=groups), :] = pick(cut, lambda q: q - a)
-    weighted = (field[...] * gwb[...]).astype(bf16)
-    sums = dot(weighted, leg[...], ((0,), (0,)))
-    tend = (sums[: 2 * vl] + parity * sums[2 * vl :]) * (live * time_step)
-    for r in range(2):
-        for h in range(2):
-            tend_out[2 * r + h] = tend[r * vl : (r + 1) * vl, h * kq : (h + 1) * kq].astype(bf16)
-    third = across(tend_out, tend_in, 2)
-    for cp in third:
-        cp.wait()
-    change = tend_in[...].reshape(levs * vl, kq)
-    move_out[...] = solve_change(change).reshape(levs, vl, kq).astype(bf16)
-    fourth = across(move_out, move_in, 3)
+        size = bands * count * groups
+        some = bands * count
+        rows32[pl.ds(0, slots * 2 * count), :] = (
+            at_slot[:, start : start + count].reshape(slots * 2 * count, lanes).astype(f32)
+        )
+        turned = swapped(
+            [
+                rows32[pl.ds(n * 2 * some + r, some, stride=2), :].astype(bf16)
+                for n in range(2)
+                for r in range(2)
+            ]
+        )
+        for a in range(groups):
+            field[pl.ds(a, some, stride=groups), :] = turned[:, a * lanes : (a + 1) * lanes]
+        weighted = (field[pl.ds(0, size), :] * gwbc[pl.ds(base, size), :]).T.astype(bf16)
+        table = legc[pl.ds(base, size), :]
+        base += size
+        if c < len(cuts) - 1:
+            sums = dot(weighted, table, ((1,), (0,)))
+            partial[...] = sums if c == 0 else partial[...] + sums
+            continue
+        for p, (first, width) in enumerate(splits):
+            cols = [slice(h * kq + first, h * kq + first + width) for h in range(2)]
+            sums = dot(
+                weighted, jnp.concatenate([table[:, q] for q in cols], axis=1), ((1,), (0,))
+            )
+            for h in range(2):
+                mine = sums[:, h * width : (h + 1) * width]
+                if c:
+                    mine = mine + partial[:, cols[h]]
+                tend = mine[: 2 * vl] + parity[:, cols[h]] * mine[2 * vl :]
+                tend = (tend * (live[:, cols[h]] * time_step)).astype(bf16)
+                for r in range(2):
+                    tend_out[2 * r + h, :, first : first + width] = tend[r * vl : (r + 1) * vl]
+            third.append(across(tend_out, tend_in, 2 + p))
+    fourth = []
+    for p, (start, count) in enumerate(splits):
+        for cp in third[p]:
+            cp.wait()
+        change = tend_in[:, :, start : start + count].reshape(levs * vl, count)
+        change = solve_change(change, damp[:, start : start + count])
+        move_out[:, :, start : start + count] = change.reshape(levs, vl, count).astype(bf16)
+        fourth.append(across(move_out, move_in, 2 + len(splits) + p))
     for cp in second:
         cp.wait()
-    for cp in fourth:
-        cp.wait()
-    for r in range(2):
-        for h in range(2):
-            out_ref[:, r, h * kq : (h + 1) * kq] = still_in[2 * r + h] + move_in[
-                2 * r + h
-            ].astype(f32)
+    for p, (start, count) in enumerate(splits):
+        for cp in fourth[p]:
+            cp.wait()
+        for r in range(2):
+            for h in range(2):
+                out_ref[:, r, h * kq + start : h * kq + start + count] = still_in[
+                    2 * r + h, :, start : start + count
+                ] + move_in[2 * r + h, :, start : start + count].astype(f32)
     for k, buf in ((0, to_grid), (1, to_slot)):
         for c in range(len(cuts)):
             await_all(buf, wave_send.at[k], c)
@@ -396,9 +447,11 @@
     lanes = 128
     groups = lanes // vl
     tiles = band // groups
-    first = tiles // 2
+    first = tiles * 3 // 5
     cuts = ((0, first), (first, tiles - first))
-    cfg = (slots, levs, half, orders, nlon, band, stride, cuts)
+    splits = ((0, kq),)
+    cfg = (slots, levs, half, orders, nlon, band, stride, cuts, splits)
+    swap = swap_blocks(groups, vl)
     vmem = pltpu.VMEM
     dma = pltpu.SemaphoreType.DMA
     cells = vmem((slots, tiles, 2, lanes), bf16)
@@ -414,7 +467,8 @@
         vmem((nmodes,), f32),
         vmem(smooth.shape, bf16),
         vmem(waves.shape, bf16),
-        dma((10,)),
+        vmem(swap.shape, bf16),
+        dma((11,)),
         dma((5,)),
         dma((2,)),
         vmem((levs, vl, kq), f32),
@@ -432,20 +486,23 @@
         vmem((half, lanes), f32),
         vmem((half, lanes), f32),
         vmem((half, lanes), f32),
+        vmem((half, lanes), f32),
+        vmem((half, orders), bf16),
+        vmem((4 * vl, orders), f32),
         vmem((nmodes, kq), f32),
         vmem((points, tiles * lanes), f32),
         vmem((points, 2 * slots), bf16),
         vmem((2 * slots, points), bf16),
         vmem((2, nmodes, 2 * nmodes), bf16),
-        dma((4, levs - 1)),
-        dma((4, levs - 1)),
+        dma((2 + 2 * len(splits), levs - 1)),
+        dma((2 + 2 * len(splits), levs - 1)),
         dma((2, len(cuts))),
         dma((2, len(cuts))),
     ]
     out = pl.pallas_call(
         functools.partial(kernel, cfg),
         out_shape=pltpu.VMEM((vl, 2, orders), f32),
-        in_specs=[pl.BlockSpec(memory_space=pl.ANY)] * 10,
+        in_specs=[pl.BlockSpec(memory_space=pl.ANY)] * 11,
         out_specs=pl.BlockSpec(memory_space=vmem),
         scratch_shapes=scratch,
         compiler_params=pltpu.CompilerParams(
@@ -463,6 +520,7 @@
         mode_rates,
         jnp.asarray(smooth),
         jnp.asarray(waves),
+        jnp.asarray(swap),
     )
     return out[None]
 

time: 42 us -> 42.6 us (1.014)
  Pallas kernels: 41 us -> 41.6 us
    pallas_call x1, Pallas kernels: 41 us -> 41.6 us  [local(): pl.pallas_call(functools.partial(kernel, cfg), out_shape=pltpu.VMEM((vl,...]
where the time goes in v3:
time: 42.6 us; the launch traced here: 42.3 us
  Pallas kernels  41.6 us (98%)
  local copies, waits for them, and re-layouts  0.73 us (2%)
    pallas_call x1, Pallas kernels, local(): pl.pallas_call(functools.partial(kernel, cfg), out_shape=pltpu.VMEM((vl,...  41.6 us

profile of v3, /device:TPU:2, one launch (start us, length us, event | category | flops | bytes accessed | tf_op | source)
XLA Modules:
  0.0 42.3 jit_solution(13879128917173036252)
XLA Ops:
  0.0 41.6 %round_trip.1 = f32[32,2,1280]{2,1,0:T(2,128)S(1)} custom-call(f32[32,2,1280]{2,1,0:T(2,128)} %bitcast.5, bf16[1280,1280]{1,0:T(8,128)(2,1)} %bitcast.4, f32[1280]{0:T(1024)} %gw_h.1, s32[64]{0:T(128)} %sw_h.1, f32[40,4096]{1,0:T(8,128)} %fac_h.1, f32[128,128]{1,0:T(8,128)} %mp_h.1, f32[128,128]{1,0:T(8,128)} %vm_h.1, f32[128]{0:T(128)} %mr_h.1, ...), custom_call_target="tpu_custom_call" | custom-call | tf_op jit(solution)/shard_map/round_trip/pallas_call | solution.py:502
  41.6 0.7 %copy.13 = f32[1,32,2,1280]{3,2,1,0:T(2,128)} copy(f32[1,32,2,1280]{3,2,1,0:T(2,128)S(1)} %bitcast.3) | data formatting | bytes 655360

commit v4 on v3

--- a/solution.py
+++ b/solution.py
@@ -120,13 +120,20 @@
     rows = 2 * tiles
 
     barrier = pltpu.get_barrier_semaphore()
+    nx, nz = 4, slots // 8
+    wx, wz, wc = lax.div(w, 2 * nz), lax.rem(lax.div(w, 2), nz), lax.rem(w, 2)
 
     def every_peer(act):
-        def step(i, _):
-            act(lax.rem(w + i, slots))
-            return 0
-
-        lax.fori_loop(1, slots, step, 0)
+        for dz in (4, 5, 3, 6, 2, 7, 1, 0):
+            first = (lax.rem(wz + dz, nz)) * 2
+            shift = 2 if dz else 0
+
+            def step(i, _):
+                x = lax.rem(wx + shift + lax.div(i, 2), nx)
+                act(x * (2 * nz) + first + lax.rem(wc + i, 2))
+                return 0
+
+            lax.fori_loop(0 if dz else 1, 2 * nx, step, 0, unroll=True)
 
     def greet(d):
         pl.semaphore_signal(barrier, inc=1, device_id=(d, y), device_id_type=MESH)
@@ -447,7 +454,7 @@
     lanes = 128
     groups = lanes // vl
     tiles = band // groups
-    first = tiles * 3 // 5
+    first = tiles // 2
     cuts = ((0, first), (first, tiles - first))
     splits = ((0, kq),)
     cfg = (slots, levs, half, orders, nlon, band, stride, cuts, splits)

time: 42.6 us -> 40.8 us (0.958)
  Pallas kernels: 41.6 us -> 39.6 us
    pallas_call x1, Pallas kernels: 41.6 us -> 39.6 us  [local(): pl.pallas_call(functools.partial(kernel, cfg), out_shape=pltpu.VMEM((vl,...]
where the time goes in v4:
time: 40.8 us; the launch traced here: 40.3 us
  Pallas kernels  39.6 us (97%)
  local copies, waits for them, and re-layouts  0.73 us (2%)
    pallas_call x1, Pallas kernels, local(): pl.pallas_call(functools.partial(kernel, cfg), out_shape=pltpu.VMEM((vl,...  39.6 us

profile of v4, /device:TPU:2, one launch (start us, length us, event | category | flops | bytes accessed | tf_op | source)
XLA Modules:
  0.0 40.3 jit_solution(1509772586370967736)
XLA Ops:
  0.0 39.6 %round_trip.1 = f32[32,2,1280]{2,1,0:T(2,128)S(1)} custom-call(f32[32,2,1280]{2,1,0:T(2,128)} %bitcast.5, bf16[1280,1280]{1,0:T(8,128)(2,1)} %bitcast.4, f32[1280]{0:T(1024)} %gw_h.1, s32[64]{0:T(128)} %sw_h.1, f32[40,4096]{1,0:T(8,128)} %fac_h.1, f32[128,128]{1,0:T(8,128)} %mp_h.1, f32[128,128]{1,0:T(8,128)} %vm_h.1, f32[128]{0:T(128)} %mr_h.1, ...), custom_call_target="tpu_custom_call" | custom-call | tf_op jit(solution)/shard_map/round_trip/pallas_call | solution.py:509
  39.6 0.7 %copy.13 = f32[1,32,2,1280]{3,2,1,0:T(2,128)} copy(f32[1,32,2,1280]{3,2,1,0:T(2,128)S(1)} %bitcast.3) | data formatting | bytes 655360

commit v5 on v4

--- a/solution.py
+++ b/solution.py
@@ -124,16 +124,12 @@
     wx, wz, wc = lax.div(w, 2 * nz), lax.rem(lax.div(w, 2), nz), lax.rem(w, 2)
 
     def every_peer(act):
-        for dz in (4, 5, 3, 6, 2, 7, 1, 0):
-            first = (lax.rem(wz + dz, nz)) * 2
-            shift = 2 if dz else 0
-
-            def step(i, _):
-                x = lax.rem(wx + shift + lax.div(i, 2), nx)
-                act(x * (2 * nz) + first + lax.rem(wc + i, 2))
-                return 0
-
-            lax.fori_loop(0 if dz else 1, 2 * nx, step, 0, unroll=True)
+        for dx in (2, 1, 3, 0):
+            for dz in (4, 5, 3, 6, 2, 7, 1, 0):
+                first = lax.rem(wx + dx, nx) * (2 * nz) + lax.rem(wz + dz, nz) * 2
+                for core in range(2):
+                    if dx or dz or core:
+                        act(first + lax.rem(wc + core, 2))
 
     def greet(d):
         pl.semaphore_signal(barrier, inc=1, device_id=(d, y), device_id_type=MESH)

time: 40.8 us -> 40.2 us (0.985)
  no operation moved by 1% of the time
where the time goes in v5:
time: 40.2 us; the launch traced here: 40.1 us
  Pallas kernels  39.4 us (98%)
  local copies, waits for them, and re-layouts  0.73 us (2%)
    pallas_call x1, Pallas kernels, local(): pl.pallas_call(functools.partial(kernel, cfg), out_shape=pltpu.VMEM((vl,...  39.4 us

profile of v5, /device:TPU:2, one launch (start us, length us, event | category | flops | bytes accessed | tf_op | source)
XLA Modules:
  0.0 40.1 jit_solution(11560744397770564457)
XLA Ops:
  0.0 39.4 %round_trip.1 = f32[32,2,1280]{2,1,0:T(2,128)S(1)} custom-call(f32[32,2,1280]{2,1,0:T(2,128)} %bitcast.5, bf16[1280,1280]{1,0:T(8,128)(2,1)} %bitcast.4, f32[1280]{0:T(1024)} %gw_h.1, s32[64]{0:T(128)} %sw_h.1, f32[40,4096]{1,0:T(8,128)} %fac_h.1, f32[128,128]{1,0:T(8,128)} %mp_h.1, f32[128,128]{1,0:T(8,128)} %vm_h.1, f32[128]{0:T(128)} %mr_h.1, ...), custom_call_target="tpu_custom_call" | custom-call | tf_op jit(solution)/shard_map/round_trip/pallas_call | solution.py:505
  39.4 0.7 %copy.13 = f32[1,32,2,1280]{3,2,1,0:T(2,128)} copy(f32[1,32,2,1280]{3,2,1,0:T(2,128)S(1)} %bitcast.3) | data formatting | bytes 655360

commit v6 on v5

--- a/solution.py
+++ b/solution.py
@@ -125,7 +125,7 @@
 
     def every_peer(act):
         for dx in (2, 1, 3, 0):
-            for dz in (4, 5, 3, 6, 2, 7, 1, 0):
+            for dz in (4, 3, 5, 2, 6, 1, 7, 0):
                 first = lax.rem(wx + dx, nx) * (2 * nz) + lax.rem(wz + dz, nz) * 2
                 for core in range(2):
                     if dx or dz or core:

time: 40.2 us -> 40.2 us (level)
  no operation moved by 1% of the time
where the time goes in v6:
time: 40.2 us; the launch traced here: 40.1 us
  Pallas kernels  39.4 us (98%)
  local copies, waits for them, and re-layouts  0.73 us (2%)
    pallas_call x1, Pallas kernels, local(): pl.pallas_call(functools.partial(kernel, cfg), out_shape=pltpu.VMEM((vl,...  39.4 us

profile of v6, /device:TPU:2, one launch (start us, length us, event | category | flops | bytes accessed | tf_op | source)
XLA Modules:
  0.0 40.1 jit_solution(17867240301667452745)
XLA Ops:
  0.0 39.4 %round_trip.1 = f32[32,2,1280]{2,1,0:T(2,128)S(1)} custom-call(f32[32,2,1280]{2,1,0:T(2,128)} %bitcast.5, bf16[1280,1280]{1,0:T(8,128)(2,1)} %bitcast.4, f32[1280]{0:T(1024)} %gw_h.1, s32[64]{0:T(128)} %sw_h.1, f32[40,4096]{1,0:T(8,128)} %fac_h.1, f32[128,128]{1,0:T(8,128)} %mp_h.1, f32[128,128]{1,0:T(8,128)} %vm_h.1, f32[128]{0:T(128)} %mr_h.1, ...), custom_call_target="tpu_custom_call" | custom-call | tf_op jit(solution)/shard_map/round_trip/pallas_call | solution.py:505
  39.4 0.7 %copy.13 = f32[1,32,2,1280]{3,2,1,0:T(2,128)} copy(f32[1,32,2,1280]{3,2,1,0:T(2,128)S(1)} %bitcast.3) | data formatting | bytes 655360
